TPU v7x, 32 devices: a whole 2x2x4 slice. The times are simulated.
32 devices in a mesh: tm: 8 (over z, y), space: 4 (over x, core).
Axes of the slice: x: 2, y: 2, z: 4, core: 2. Of those that a mesh axis runs over, the one named last changes fastest.
Arguments:
- snapshots: bfloat16 [4096, 3, 4096], P('tm', None, 'space'), may hold values from -6 to 6
- cell_weights: float32 [4096], P('space'), may hold values from 0.25 to 4
- triads: int32 [64, 3], replicated, may hold values from 0 to 127, as said below
- owner_slots: int32 [8, 16], replicated, may hold values from -1 to 63, as said below
Outputs:
- bispectra: float32 [128, 512], P(('tm', 'space'))
Inputs may be any that keep to these rules, and one draw needn't show every extreme that they name: `triads`: every row is (k, l, k + l); all three entries are below 128. `owner_slots`: every triad index stands in exactly one slot of the table; in each row the used slots come first and the others hold -1; some owner fills all 16 slots.
All inputs are finite; a program needn't handle non-finite values.
Results may differ from a plain program's by a relative error of at most 0.0076.
Values may be sent and summed in bfloat16 or wider, within the bound.
A program may use at most 64 MiB of HBM per device.

v0:
```python
import math
import jax
import jax.numpy as jnp
from jax import lax
from jax.sharding import PartitionSpec as P

NB = 16
NT = 256
K = 128


def spectral_table():
    sample = jnp.arange(NT, dtype=jnp.int32)
    freq_bins = jnp.arange(K, dtype=jnp.int32)
    phase_idx = freq_bins[:, None] * sample[None, :] % NT
    angles = 2.0 * math.pi / NT * phase_idx.astype(jnp.float32)
    window = 0.5 - 0.5 * jnp.cos(2.0 * math.pi / NT * sample.astype(jnp.float32))
    norm_scale = math.sqrt(8.0 / (3.0 * NT))
    real_rows = norm_scale * window[None, :] * jnp.cos(angles)
    imag_rows = -norm_scale * window[None, :] * jnp.sin(angles)
    return jnp.stack([real_rows, imag_rows], axis=1).reshape(2 * K, NT).astype(jnp.bfloat16)


def transform(piece):
    snap_total, item_count, cell_count = piece.shape
    blocks = piece.reshape(NB, NT, item_count * cell_count)
    spectra = jnp.einsum(
        "jn,bnc->jbc", spectral_table(), blocks, preferred_element_type=jnp.float32
    )
    return spectra.astype(jnp.bfloat16).reshape(K, 2, NB, item_count, cell_count)


def triad_terms(spectra, weight_rows, triads, triad_index):
    count = triad_index.shape[0]
    lane_total = weight_rows.shape[0]
    triad_freqs = jnp.take(triads, triad_index, axis=0)
    first_spec = (
        jnp.take(spectra, triad_freqs[:, 0], axis=0)
        .reshape(count, 2, NB, lane_total)
        .astype(jnp.float32)
    )
    second_spec = (
        jnp.take(spectra, triad_freqs[:, 1], axis=0)
        .reshape(count, 2, NB, lane_total)
        .astype(jnp.float32)
    )
    third_spec = jnp.take(spectra, triad_freqs[:, 2], axis=0).reshape(count, 2, NB, lane_total)
    prod_real = (
        first_spec[:, 0] * second_spec[:, 0] - first_spec[:, 1] * second_spec[:, 1]
    ) * weight_rows
    prod_imag = (
        first_spec[:, 0] * second_spec[:, 1] + first_spec[:, 1] * second_spec[:, 0]
    ) * weight_rows
    product = jnp.stack([prod_real, prod_imag], axis=1).astype(jnp.bfloat16)
    gram = jnp.einsum("trbc,tsdc->trbsd", product, third_spec, preferred_element_type=jnp.float32)
    bis_real = gram[:, 0, :, 0, :] + gram[:, 1, :, 1, :]
    bis_imag = gram[:, 0, :, 1, :] - gram[:, 1, :, 0, :]
    return jnp.stack([bis_real, bis_imag], axis=1).reshape(count, 2 * NB * NB)


def block_size(amount, quantum):
    return quantum * math.gcd(amount // quantum, max(1, 64 // quantum))


def blocked(index_list, quantum, spectra, weight_rows, triads):
    amount = index_list.shape[0]
    width_blk = block_size(amount, quantum)
    grouped = index_list.reshape(amount // width_blk, width_blk)

    def group_terms(slot_group):
        filled = (slot_group >= 0).astype(jnp.float32)
        return (
            triad_terms(spectra, weight_rows, triads, jnp.maximum(slot_group, 0)) * filled[:, None]
        )

    return lax.map(group_terms, grouped).reshape(amount, 2 * NB * NB)


def shards(snapshots, cell_weights, triads, owner_slots):
    spectra = transform(lax.all_to_all(snapshots, "tm", split_axis=2, concat_axis=0, tiled=True))
    cell_count = spectra.shape[4]
    spectra = spectra.reshape(K, 2 * NB * 3 * cell_count)
    tm_total = lax.axis_size("tm")
    space_total = lax.axis_size("space")
    device_total = tm_total * space_total
    weight_scale = 1.0 / math.sqrt(3.0 * cell_count * device_total)
    local_w = (
        lax.dynamic_slice_in_dim(cell_weights, lax.axis_index("tm") * cell_count, cell_count, 0)
        * weight_scale
    )
    weight_rows = jnp.tile(local_w, 3)
    flat_slots = owner_slots.reshape(-1)
    my_rows = flat_slots.shape[0] // device_total
    return lax.psum_scatter(
        blocked(flat_slots, my_rows, spectra, weight_rows, triads),
        ("tm", "space"),
        scatter_dimension=0,
        tiled=True,
    )


def solution(mesh):
    placed = (P("tm", None, "space"), P("space"), P(), P())
    return jax.shard_map(
        shards, mesh=mesh, in_specs=placed, out_specs=P(("tm", "space"), None), check_vma=False
    )
```

profile of v0, /device:TPU:0, one launch (start us, length us, event | category | flops | bytes accessed | tf_op | source)
XLA Modules:
  0.0 327.5 jit_solution(2348501136595664732)
XLA Ops:
  6.5 7.7 %copy.36 = bf16[512,3,1024]{0,1,2:T(4,128)(2,1)} copy(bf16[512,3,1024]{2,0,1:T(8,128)(2,1)} %param.8) | data formatting | bytes 6291456 | tf_op args[0]
  14.2 7.4 %all-to-all-start = ((bf16[512,3,1024]{0,1,2:T(4,128)(2,1)}), bf16[512,3,1024]{0,1,2:T(4,128)(2,1)}, u32[]{:S(2)}, u32[]{:S(2)}) async-start(bf16[512,3,1024]{0,1,2:T(4,128)(2,1)} %copy.36), calls=%async_computation | async-start | bytes 8388608 | tf_op jit(solution)/shard_map/all_to_all | solution.py:80
  23.5 91.4 %all-to-all-done = bf16[512,3,1024]{0,1,2:T(4,128)(2,1)} async-done(((bf16[512,3,1024]{0,1,2:T(4,128)(2,1)}), bf16[512,3,1024]{0,1,2:T(4,128)(2,1)}, u32[]{:S(2)}, u32[]{:S(2)}) %all-to-all-start) | async-done | bytes 3145760 | tf_op jit(solution)/shard_map/all_to_all | solution.py:80
  114.9 4.5 %copy.54 = bf16[512,3,8,128]{0,2,3,1:T(8,128)(2,1)S(1)} copy(bf16[512,3,8,128]{0,1,3,2:T(4,128)(2,1)} %bitcast) | data formatting | bytes 6291456 | tf_op jit(solution)/shard_map/all_to_all | solution.py:80
  119.4 3.4 %reshape.253 = bf16[16,256,384]{1,0,2:T(8,128)(2,1)} reshape(bf16[8,512,3,128]{1,0,3,2:T(8,128)(2,1)S(1)} %bitcast.74) | data formatting | bytes 6291456 | tf_op jit(solution)/shard_map/reshape | solution.py:26
  122.7 4.2 %fusion.12 = bf16[256,16,384]{2,0,1:T(8,128)(2,1)S(1)} fusion(bf16[256,256,1]{1,0,2:T(8,128)(2,1)S(1)} %reshape.310, bf16[16,256,384]{1,0,2:T(8,128)(2,1)} %reshape.253), kind=kOutput, calls=%fused_computation.46 | convolution fusion | flops 806879232 | bytes 6422528 | tf_op jit(solution)/shard_map/jn,bnc->jbc/dot_general | solution.py:27
  127.0 3.5 %copy.39 = bf16[256,16,384]{2,1,0:T(8,128)(2,1)} copy(bf16[256,16,384]{2,0,1:T(8,128)(2,1)S(1)} %fusion.12) | data formatting | bytes 6291456 | tf_op jit(solution)/shard_map/convert_element_type | solution.py:30
  130.5 4.2 %reshape_reshape.7 = bf16[128,12288]{1,0:T(8,128)(2,1)S(1)} reshape(bf16[256,16,384]{2,1,0:T(8,128)(2,1)} %copy.39) | data formatting | bytes 6291456 | tf_op jit(solution)/shard_map/reshape;reshape | solution.py:82
  134.7 60.4 %while.11 = (s32[]{:T(128)}, f32[2,64,512]{2,1,0:T(8,128)}, s32[2,64]{1,0:T(2,128)S(1)}, s32[64,3]{1,0:T(8,128)S(1)}, bf16[128,12288]{1,0:T(8,128)(2,1)S(1)}, /*index=5*/f32[128]{0:T(128)S(1)}, s32[]{:T(128)}) while((s32[]{:T(128)}, f32[2,64,512]{2,1,0:T(8,128)}, s32[2,64]{1,0:T(2,128)S(1)}, s32[64,3]{1,0:T(8,128)S(1)}, ...), condition=%wide.region_1.3_spmd.clone, body=%wide.region_0.2_spmd.clone.sunk | while | flops 61446336 | bytes 69630632 | solution.py:76
  135.7 2.7 gather_fusion.1
  138.4 1.7 select_convert_fusion.4
  140.0 2.2 copy.61
  142.3 2.7 gather_fusion.2
  148.5 1.7 multiply_convert_fusion.5
  150.2 2.7 gather_fusion.3
  155.9 2.9 fusion.30
  165.9 2.7 gather_fusion.1
  168.6 1.7 select_convert_fusion.4
  170.2 2.2 copy.61
  172.5 2.7 gather_fusion.2
  178.7 1.7 multiply_convert_fusion.5
  180.4 2.7 gather_fusion.3
  186.1 2.9 fusion.30
  195.1 124.2 %all-reduce.3.cloned.1.call-done = f32[128,512]{1,0:T(8,128)} async-done(((f32[128,512]{1,0:T(8,128)}), f32[128,512]{1,0:T(8,128)}) %all-reduce.3.cloned.1.call-update) | async-done | bytes 262160
  (79 shorter events, 30.2 us)
Async XLA Ops:
  14.2 8.4 %copy-start.4 = (s32[64,3]{0,1:T(4,128)S(1)}, s32[64,3]{0,1:T(4,128)}, u32[]{:S(2)}) copy-start(s32[64,3]{0,1:T(4,128)} %param.10) | copy-start | bytes 2308
  14.2 8.5 %copy-start.3 = (s32[8,16]{1,0:T(8,128)S(1)}, s32[8,16]{1,0:T(8,128)}, u32[]{:S(2)}) copy-start(s32[8,16]{1,0:T(8,128)} %param.11) | copy-start | bytes 1540
  14.2 100.7 %all-to-all-start = ((bf16[512,3,1024]{0,1,2:T(4,128)(2,1)}), bf16[512,3,1024]{0,1,2:T(4,128)(2,1)}, u32[]{:S(2)}, u32[]{:S(2)}) async-start(bf16[512,3,1024]{0,1,2:T(4,128)(2,1)} %copy.36), calls=%async_computation | async-start | bytes 8388608 | tf_op jit(solution)/shard_map/all_to_all | solution.py:80
  21.6 297.7 %all-reduce.3.cloned.1.call-start = ((), (), s32[]{:S(2)}) async-start(), calls=%async_computation.1 | async-start | bytes 524288
  146.6 1.9 copy-start
  154.5 1.1 copy-start.1
  154.5 1.4 copy-start.2
  176.8 1.9 copy-start
  184.7 1.1 copy-start.1
  184.8 1.4 copy-start.2
Sparse Core Ops, SparseCore 0:
  195.3 124.0 all-reduce.2
where the time goes:
time: 329 us; the launch traced here: 328 us
  waiting for transfers between devices  216 us (66%)
  local copies, waits for them, and re-layouts  63.2 us (19%)
  other arithmetic  17.4 us (5%)
  between operations  13.5 us (4%)
  matrix products  10.1 us (3%)
  starting transfers between devices  7.45 us (2%)
    unnamed x2, waiting for transfers between devices  124 us
    all_to_all x1, waiting for transfers between devices, shards(): lax.all_to_all(snapshots, 'tm', split_axis=2, concat_axis=0, tiled=True)  91.4 us
    while x18, local copies, waits for them, and re-layouts  10.8 us
    unnamed x7, local copies, waits for them, and re-layouts  9.08 us
    all_to_all x1, starting transfers between devices, shards(): lax.all_to_all(snapshots, 'tm', split_axis=2, concat_axis=0, tiled=True)  7.41 us
  transfers between devices with their start and end apart: 2, of which 2 were waited for; matrix products, arithmetic and copies ran while one was open for 1% of the time, Pallas kernels for 0%

commit v1 on v0

--- a/solution.py
+++ b/solution.py
@@ -7,6 +7,29 @@
 NB = 16
 NT = 256
 K = 128
+
+
+def in_blocks(x, dim, length):
+    shape = x.shape
+    blocks = x.reshape(*shape[:dim], length, shape[dim] // length, *shape[dim + 1 :])
+    return jnp.moveaxis(blocks, dim, 0)
+
+
+def joined_along(parts, dim):
+    parts = jnp.moveaxis(parts, 0, dim)
+    shape = parts.shape
+    return parts.reshape(*shape[:dim], shape[dim] * shape[dim + 1], *shape[dim + 2 :])
+
+
+def sent_to_each(value, axis, split_dim, concat_dim):
+    size, index = (lax.axis_size(axis), lax.axis_index(axis))
+    blocks = in_blocks(value, split_dim, size)
+    outs = [blocks[index]]
+    for hop in range(1, size):
+        sent = blocks[(index + hop) % size]
+        outs.append(lax.ppermute(sent, axis, [(i, (i + hop) % size) for i in range(size)]))
+    blocks = jnp.stack(outs)[(index - jnp.arange(size)) % size]
+    return joined_along(blocks, concat_dim)
 
 
 def spectral_table():
@@ -77,7 +100,7 @@
 
 
 def shards(snapshots, cell_weights, triads, owner_slots):
-    spectra = transform(lax.all_to_all(snapshots, "tm", split_axis=2, concat_axis=0, tiled=True))
+    spectra = transform(sent_to_each(snapshots, "tm", 2, 0))
     cell_count = spectra.shape[4]
     spectra = spectra.reshape(K, 2 * NB * 3 * cell_count)
     tm_total = lax.axis_size("tm")

time: 329 us -> 308 us (0.936)
  waiting for transfers between devices: 216 us -> 171 us
  local copies, waits for them, and re-layouts: 63.2 us -> 82.2 us
  starting transfers between devices: 7.45 us -> 16.2 us
    all_to_all x1 -> x0, waiting for transfers between devices: 91.4 us -> none  [shards(): lax.all_to_all(snapshots, 'tm', split_axis=2, concat_axis=0, tiled=True)]
    ppermute x0 -> x7, waiting for transfers between devices: none -> 25.2 us  [sent_to_each(): lax.ppermute(sent, axis, [(i, (i + hop) % size) for i in range(size)])]
    another operation x0 -> x12, local copies, waits for them, and re-layouts: none -> 22 us  [the longest x2 12.3 us: transform(): blocks = piece.reshape(NB, NT, item_count * cell_count)]
    unnamed x2, waiting for transfers between devices: 124 us -> 145 us
    ppermute x0 -> x7, starting transfers between devices: none -> 16.2 us  [sent_to_each(): lax.ppermute(sent, axis, [(i, (i + hop) % size) for i in range(size)])]
    all_to_all x1 -> x0, starting transfers between devices: 7.41 us -> none  [shards(): lax.all_to_all(snapshots, 'tm', split_axis=2, concat_axis=0, tiled=True)]
    all_to_all x1 -> x0, local copies, waits for them, and re-layouts: 4.48 us -> none  [shards(): lax.all_to_all(snapshots, 'tm', split_axis=2, concat_axis=0, tiled=True)]
    unnamed x7 -> x20, local copies, waits for them, and re-layouts: 9.08 us -> 13 us
  transfers between devices with their start and end apart: 2 -> 8, of which waited for: 2 -> 4; matrix products, arithmetic and copies ran while one was open for 1% -> 5% of each run, Pallas kernels for 0% -> 0%
where the time goes in v1:
time: 308 us; the launch traced here: 307 us
  waiting for transfers between devices  171 us (56%)
  local copies, waits for them, and re-layouts  82.2 us (27%)
  other arithmetic  17.6 us (6%)
  starting transfers between devices  16.2 us (5%)
  between operations  13.6 us (4%)
  matrix products  6.88 us (2%)
    unnamed x2, waiting for transfers between devices  145 us
    ppermute x7, waiting for transfers between devices, sent_to_each(): lax.ppermute(sent, axis, [(i, (i + hop) % size) for i in range(size)])  25.2 us
    ppermute x7, starting transfers between devices, sent_to_each(): lax.ppermute(sent, axis, [(i, (i + hop) % size) for i in range(size)])  16.2 us
    unnamed x20, local copies, waits for them, and re-layouts  13 us
    another operation x2, local copies, waits for them, and re-layouts, transform(): blocks = piece.reshape(NB, NT, item_count * cell_count)  12.3 us
    another operation x9, local copies, waits for them, and re-layouts  8.86 us
    while x18, local copies, waits for them, and re-layouts  8.66 us
  transfers between devices with their start and end apart: 8, of which 4 were waited for; matrix products, arithmetic and copies ran while one was open for 5% of the time, Pallas kernels for 0%

profile of v1, /device:TPU:0, one launch (start us, length us, event | category | flops | bytes accessed | tf_op | source)
XLA Modules:
  0.0 307.3 jit_solution(1680732654775428275)
XLA Ops:
  6.5 3.2 %copy.68 = bf16[512,3,1024]{0,2,1:T(8,128)(2,1)S(1)} copy(bf16[512,3,1024]{2,0,1:T(8,128)(2,1)} %param.8) | data formatting | bytes 6291456 | tf_op args[0]
  13.4 3.0 collective-permute-start
  21.1 2.6 collective-permute-start.2
  26.4 2.7 collective-permute-start.4
  35.6 3.7 %collective-permute-start.6 = (bf16[512,3,128]{2,0,1:T(8,128)(2,1)S(1)}, bf16[512,3,128]{2,0,1:T(8,128)(2,1)S(1)}, u32[]{:S(2)}, u32[]{:S(2)}) collective-permute-start(bf16[512,3,128]{2,0,1:T(8,128)(2,1)S(1)} %bitcast.97), channel_id=1, source_target_pairs={{0,28},{4,0},{8,4},{12,8},{16,12},{20,16},{24,20},{28,24},{1,29},{... | collective-permute-start | bytes 1179656 | tf_op jit(solution)/shard_map/ppermute | solution.py:30
  41.1 21.6 %collective-permute-done.2 = bf16[512,3,128]{2,0,1:T(8,128)(2,1)} collective-permute-done((bf16[512,3,128]{2,0,1:T(8,128)(2,1)S(1)}, bf16[512,3,128]{2,0,1:T(8,128)(2,1)}, u32[]{:S(2)}, u32[]{:S(2)}) %collective-permute-start.2) | collective-permute-done | bytes 393248 | tf_op jit(solution)/shard_map/ppermute | solution.py:30
  67.1 3.3 %collective-permute-done.6 = bf16[512,3,128]{2,0,1:T(8,128)(2,1)S(1)} collective-permute-done((bf16[512,3,128]{2,0,1:T(8,128)(2,1)S(1)}, bf16[512,3,128]{2,0,1:T(8,128)(2,1)S(1)}, u32[]{:S(2)}, u32[]{:S(2)}) %collective-permute-start.6) | collective-permute-done | bytes 393248 | tf_op jit(solution)/shard_map/ppermute | solution.py:30
  71.1 3.0 gather_fusion.4
  74.2 4.7 %copy.84 = bf16[8,512,3,128]{3,2,1,0:T(4,128)(2,1)} copy(bf16[8,512,3,128]{3,1,2,0:T(8,128)(2,1)S(1)} %gather_fusion.4) | data formatting | bytes 6291456 | tf_op jit(solution)/shard_map/reshape;reshape | solution.py:49
  78.8 7.7 %reshape.383 = bf16[16,256,384]{2,1,0:T(8,128)(2,1)S(1)} reshape(bf16[8,512,3,128]{3,2,1,0:T(4,128)(2,1)} %copy.84) | data formatting | bytes 6291456 | tf_op jit(solution)/shard_map/reshape;reshape | solution.py:49
  87.5 3.5 %copy.79 = bf16[256,16,384]{2,1,0:T(8,128)(2,1)} copy(bf16[256,16,384]{2,0,1:T(8,128)(2,1)S(1)} %convolution_convert_fusion) | data formatting | bytes 6291456 | tf_op jit(solution)/shard_map/convert_element_type | solution.py:53
  91.0 4.2 %reshape_reshape.11 = bf16[128,12288]{1,0:T(8,128)(2,1)S(1)} reshape(bf16[256,16,384]{2,1,0:T(8,128)(2,1)} %copy.79) | data formatting | bytes 6291456 | tf_op jit(solution)/shard_map/reshape;reshape | solution.py:105
  95.2 58.5 %while.11 = (s32[]{:T(128)}, f32[2,64,512]{2,1,0:T(8,128)}, s32[2,64]{1,0:T(2,128)S(1)}, s32[64,3]{1,0:T(8,128)S(1)}, bf16[128,12288]{1,0:T(8,128)(2,1)S(1)}, /*index=5*/f32[128]{0:T(128)S(1)}, s32[]{:T(128)}) while((s32[]{:T(128)}, f32[2,64,512]{2,1,0:T(8,128)}, s32[2,64]{1,0:T(2,128)S(1)}, s32[64,3]{1,0:T(8,128)S(1)}, ...), condition=%wide.region_1.3_spmd.clone, body=%wide.region_0.2_spmd.clone.sunk | while | flops 61446336 | bytes 69630632 | solution.py:99
  96.2 2.7 gather_fusion.1
  100.5 2.2 copy.97
  102.8 2.7 gather_fusion.2
  110.7 2.7 gather_fusion.3
  115.4 2.9 fusion.28
  125.4 2.7 gather_fusion.1
  129.8 2.2 copy.97
  132.0 2.7 gather_fusion.2
  139.9 2.7 gather_fusion.3
  144.7 2.9 fusion.28
  153.7 145.5 %all-reduce.3.cloned.1.call-done = f32[128,512]{1,0:T(8,128)} async-done(((f32[128,512]{1,0:T(8,128)}), f32[128,512]{1,0:T(8,128)}) %all-reduce.3.cloned.1.call-update) | async-done | bytes 262160
  (117 shorter events, 58.7 us)
Async XLA Ops:
  6.5 292.6 %all-reduce.3.cloned.1.call-start = ((), (), s32[]{:S(2)}) async-start(), calls=%async_computation | async-start | bytes 524288
  11.4 14.9 %copy-start.5 = (bf16[512,3,1,128]{0,3,2,1:T(8,128)(2,1)S(1)}, bf16[512,3,1,128]{0,3,2,1:T(8,128)(2,1)}, u32[]{:S(2)}) copy-start(bf16[512,3,1,128]{0,3,2,1:T(8,128)(2,1)} %get-tuple-element.117) | copy-start | bytes 1179652
  11.4 17.9 %copy-start.4 = (bf16[512,3,1,128]{0,3,2,1:T(8,128)(2,1)S(1)}, bf16[512,3,1,128]{0,3,2,1:T(8,128)(2,1)}, u32[]{:S(2)}) copy-start(bf16[512,3,1,128]{0,3,2,1:T(8,128)(2,1)} %get-tuple-element.122) | copy-start | bytes 1179652
  11.4 20.2 %copy-start.3 = (bf16[512,3,1,128]{0,3,2,1:T(8,128)(2,1)S(1)}, bf16[512,3,1,128]{0,3,2,1:T(8,128)(2,1)}, u32[]{:S(2)}) copy-start(bf16[512,3,1,128]{0,3,2,1:T(8,128)(2,1)} %get-tuple-element.116) | copy-start | bytes 1179652
  13.4 19.1 %collective-permute-start = (bf16[512,3,128]{2,0,1:T(8,128)(2,1)}, bf16[512,3,128]{2,0,1:T(8,128)(2,1)}, u32[]{:S(2)}, u32[]{:S(2)}) collective-permute-start(bf16[512,3,128]{2,0,1:T(8,128)(2,1)} %bitcast.2), channel_id=1, source_target_pairs={{0,4},{4,8},{8,12},{12,16},{16,20},{20,24},{24,28},{28,0},{1,5},{5... | collective-permute-start | bytes 1179656 | tf_op jit(solution)/shard_map/ppermute | solution.py:30
  18.3 17.4 %collective-permute-start.1 = (bf16[512,3,128]{2,0,1:T(8,128)(2,1)}, bf16[512,3,128]{2,0,1:T(8,128)(2,1)}, u32[]{:S(2)}, u32[]{:S(2)}) collective-permute-start(bf16[512,3,128]{2,0,1:T(8,128)(2,1)} %bitcast.4), channel_id=1, source_target_pairs={{0,8},{4,12},{8,16},{12,20},{16,24},{20,28},{24,0},{28,4},{1,9},{5... | collective-permute-start | bytes 1179656 | tf_op jit(solution)/shard_map/ppermute | solution.py:30
  19.9 12.4 %copy-start.7 = (s32[64,3]{0,1:T(4,128)S(1)}, s32[64,3]{0,1:T(4,128)}, u32[]{:S(2)}) copy-start(s32[64,3]{0,1:T(4,128)} %param.10) | copy-start | bytes 2308
  19.9 12.5 %copy-start.6 = (s32[8,16]{1,0:T(8,128)S(1)}, s32[8,16]{1,0:T(8,128)}, u32[]{:S(2)}) copy-start(s32[8,16]{1,0:T(8,128)} %param.11) | copy-start | bytes 1540
  21.1 41.5 %collective-permute-start.2 = (bf16[512,3,128]{2,0,1:T(8,128)(2,1)S(1)}, bf16[512,3,128]{2,0,1:T(8,128)(2,1)}, u32[]{:S(2)}, u32[]{:S(2)}) collective-permute-start(bf16[512,3,128]{2,0,1:T(8,128)(2,1)S(1)} %bitcast.96), channel_id=1, source_target_pairs={{0,12},{4,16},{8,20},{12,24},{16,28},{20,0},{24,4},{28,8},{1,13},{... | collective-permute-start | bytes 1179656 | tf_op jit(solution)/shard_map/ppermute | solution.py:30
  24.9 39.9 %collective-permute-start.3 = (bf16[512,3,128]{2,0,1:T(8,128)(2,1)S(1)}, bf16[512,3,128]{2,0,1:T(8,128)(2,1)S(1)}, u32[]{:S(2)}, u32[]{:S(2)}) collective-permute-start(bf16[512,3,128]{2,0,1:T(8,128)(2,1)S(1)} %bitcast.95), channel_id=1, source_target_pairs={{0,16},{4,20},{8,24},{12,28},{16,0},{20,4},{24,8},{28,12},{1,17},{... | collective-permute-start | bytes 1179656 | tf_op jit(solution)/shard_map/ppermute | solution.py:30
  26.4 39.1 %collective-permute-start.4 = (bf16[512,3,128]{2,0,1:T(8,128)(2,1)S(1)}, bf16[512,3,128]{2,0,1:T(8,128)(2,1)S(1)}, u32[]{:S(2)}, u32[]{:S(2)}) collective-permute-start(bf16[512,3,128]{2,0,1:T(8,128)(2,1)S(1)} %bitcast.94), channel_id=1, source_target_pairs={{0,20},{4,24},{8,28},{12,0},{16,4},{20,8},{24,12},{28,16},{1,21},{... | collective-permute-start | bytes 1179656 | tf_op jit(solution)/shard_map/ppermute | solution.py:30
  32.5 33.8 %collective-permute-start.5 = (bf16[512,3,128]{2,0,1:T(8,128)(2,1)S(1)}, bf16[512,3,128]{2,0,1:T(8,128)(2,1)S(1)}, u32[]{:S(2)}, u32[]{:S(2)}) collective-permute-start(bf16[512,3,128]{2,0,1:T(8,128)(2,1)S(1)} %bitcast.98), channel_id=1, source_target_pairs={{0,24},{4,28},{8,0},{12,4},{16,8},{20,12},{24,16},{28,20},{1,25},{... | collective-permute-start | bytes 1179656 | tf_op jit(solution)/shard_map/ppermute | solution.py:30
  35.6 34.7 %collective-permute-start.6 = (bf16[512,3,128]{2,0,1:T(8,128)(2,1)S(1)}, bf16[512,3,128]{2,0,1:T(8,128)(2,1)S(1)}, u32[]{:S(2)}, u32[]{:S(2)}) collective-permute-start(bf16[512,3,128]{2,0,1:T(8,128)(2,1)S(1)} %bitcast.97), channel_id=1, source_target_pairs={{0,28},{4,0},{8,4},{12,8},{16,12},{20,16},{24,20},{28,24},{1,29},{... | collective-permute-start | bytes 1179656 | tf_op jit(solution)/shard_map/ppermute | solution.py:30
  107.1 1.9 copy-start
  113.4 2.0 copy-start.1
  113.4 2.0 copy-start.2
  136.4 1.9 copy-start
  142.6 2.0 copy-start.1
  142.6 2.0 copy-start.2
Sparse Core Ops, SparseCore 0:
  153.8 145.2 all-reduce.2
